TPU v7x, 32 devices: a whole 2x2x4 slice. The times are simulated.
32 devices in a mesh: crop: 2 (over y), row: 4 (over x, core), col: 4 (over z).
Axes of the slice: x: 2, y: 2, z: 4, core: 2. Of those that a mesh axis runs over, the one named last changes fastest.
Arguments:
- pair: bfloat16 [1536, 768, 128], P(('crop', 'col'), 'row'), parts along dimension 0, may hold values from -40 to 40
- chain_ids: int32 [1536], P('crop'), parts along dimension 0, may hold values from 0 to 3, never falling along the last dimension, each value on 1 to 384 neighbouring positions
- block_keep: int32 [12, 6], P('crop'), parts along dimension 0, may hold values 0 or 1
- norm_gain: float32 [128], replicated, may hold values from 0.1 to 1.9
- norm_bias: float32 [128], replicated, may hold values from -3 to 3
- left_weight: bfloat16 [128, 256], replicated, may hold values from -0.5 to 0.5
- right_weight: bfloat16 [128, 256], replicated, may hold values from -0.5 to 0.5
- gate_weight: bfloat16 [128, 128], replicated, may hold values from -0.5 to 0.5
- out_gain: float32 [128], replicated, may hold values from 0.1 to 1.9
- out_bias: float32 [128], replicated, may hold values from -3 to 3
- out_weight: bfloat16 [128, 128], replicated, may hold values from -0.5 to 0.5
Outputs:
- update: bfloat16 [1536, 768, 128], P(('crop', 'col'), 'row'), parts along dimension 0
There are 2 independent parts, one for each index of `crop`. A program takes and returns all parts, laid end to end along the dimension named above; an argument that names none is the same for every part. Nothing has to cross between parts.
Inputs may be any that keep to these rules, and one draw needn't show every extreme that they name: `chain_ids`: chain ids never fall along the crop; every one of the 4 chains holds 1 to 384 tokens, one of them exactly that many.
All inputs are finite; a program needn't handle non-finite values.
Results may differ from a plain program's by a relative error of at most 0.0095.
Values may be sent and summed in bfloat16 or wider, within the bound.
A program may use at most 448 MiB of HBM per device.

v0:
```python
import jax
import jax.numpy as jnp
from jax import lax
from jax.sharding import PartitionSpec as P

BLOCK = 128


def layer_norm(values, gain, bias):
    mean = jnp.mean(values, axis=-1, keepdims=True)
    centered = values - mean
    spread = jnp.mean(centered * centered, axis=-1, keepdims=True)
    return centered * lax.rsqrt(spread + 1e-05) * gain + bias


def gated_projection(normed, weight, mask):
    hidden = weight.shape[1] // 2
    both = jnp.dot(normed.reshape(-1, normed.shape[-1]), weight, preferred_element_type=jnp.float32)
    both = both.reshape(normed.shape[:-1] + (2 * hidden,))
    return (mask[..., None] * jax.nn.sigmoid(both[..., hidden:]) * both[..., :hidden]).astype(
        jnp.bfloat16
    )


def block_table(start, count, blocks):
    positions = start + lax.iota(jnp.int32, count)
    return ((positions // BLOCK)[:, None] == lax.iota(jnp.int32, blocks)[None, :]).astype(
        jnp.float32
    )


def pair_mask(chain_ids, keep_table, row_start, row_count, col_start, col_count):
    row_chain = lax.dynamic_slice_in_dim(chain_ids, row_start, row_count)
    col_chain = lax.dynamic_slice_in_dim(chain_ids, col_start, col_count)
    blocks = keep_table.shape[0]
    left_table = block_table(row_start, row_count, blocks)
    right_table = block_table(col_start, col_count, blocks)
    kept = jnp.dot(jnp.dot(left_table, keep_table), right_table.T)
    return jnp.where(row_chain[:, None] == col_chain[None, :], jnp.ones_like(kept), kept)


def shards(
    pair,
    chain_ids,
    block_keep,
    norm_gain,
    norm_bias,
    left_weight,
    right_weight,
    gate_weight,
    out_gain,
    out_bias,
    out_weight,
):
    tile_rows, tile_cols, channels = pair.shape
    hidden = left_weight.shape[1] // 2
    row_start = lax.axis_index("col") * tile_rows
    col_start = lax.axis_index("row") * tile_cols
    keep_table = block_keep.astype(jnp.float32)
    normed = layer_norm(pair.astype(jnp.float32), norm_gain, norm_bias).astype(jnp.bfloat16)
    local_mask = pair_mask(chain_ids, keep_table, row_start, tile_rows, col_start, tile_cols)
    left = gated_projection(normed, left_weight, local_mask)
    piece = lax.all_gather(normed, "col", axis=0, tiled=True)
    piece_mask = pair_mask(
        chain_ids, keep_table, jnp.int32(0), piece.shape[0], col_start, tile_cols
    )
    right_all = gated_projection(piece, right_weight, piece_mask)
    summed = lax.psum_scatter(
        jnp.einsum("jkh,ikh->jih", right_all, left, preferred_element_type=jnp.float32).astype(
            jnp.bfloat16
        ),
        "row",
        scatter_dimension=0,
        tiled=True,
    ).astype(jnp.float32)
    out_normed = jnp.swapaxes(layer_norm(summed, out_gain, out_bias).astype(jnp.bfloat16), 0, 1)
    gate = jax.nn.sigmoid(
        jnp.dot(normed.reshape(-1, channels), gate_weight, preferred_element_type=jnp.float32)
    )
    projected = jnp.dot(
        out_normed.reshape(-1, hidden), out_weight, preferred_element_type=jnp.float32
    )
    return (gate * projected).reshape(tile_rows, tile_cols, channels).astype(jnp.bfloat16)


def solution(mesh):
    placed = (
        P(("crop", "col"), "row", None),
        P("crop"),
        P("crop", None),
        P(),
        P(),
        P(),
        P(),
        P(),
        P(),
        P(),
        P(),
    )
    return jax.shard_map(
        shards,
        mesh=mesh,
        in_specs=placed,
        out_specs=P(("crop", "col"), "row", None),
        check_vma=False,
    )
```

profile of v0, /device:TPU:8, one launch (start us, length us, event | category | flops | bytes accessed | tf_op | source)
XLA Modules:
  0.0 1261.7 jit_solution(17507582710629630678)
XLA Ops:
  6.5 13.9 %convert_reduce_fusion.1 = f32[192,192]{0,1:T(8,128)S(1)} fusion(bf16[192,192,128]{2,1,0:T(8,128)(2,1)} %param.11), kind=kLoop, calls=%fused_computation.17 | loop fusion | flops 9400320 | bytes 9584640 | tf_op jit(solution)/shard_map/reduce_sum | solution.py:10
  20.5 0.0 copy-start.4
  20.5 0.0 copy-start.5
  20.5 0.0 copy-start.2
  20.5 14.0 %fusion.17 = f32[192,192]{0,1:T(8,128)S(1)} fusion(f32[192,192]{0,1:T(8,128)S(1)} %broadcast_multiply_fusion.1, bf16[192,192,128]{2,1,0:T(8,128)(2,1)} %param.11), kind=kLoop, calls=%fused_computation.26 | loop fusion | flops 18837504 | bytes 9732096 | tf_op jit(solution)/shard_map/reduce_sum | solution.py:12
  34.6 13.7 %fusion.20 = bf16[192,192,128]{2,0,1:T(8,128)(2,1)} fusion(f32[128]{0:T(128)S(1)} %copy-done.6, f32[128]{0:T(128)S(1)} %copy-done.7, f32[192,192]{0,1:T(8,128)S(1)} %add_rsqrt_fusion.1, f32[192,192]{0,1:T(8,128)S(1)} %broadcast_multiply_fusion.1, bf16[192,192,128]{2,1,0:T(8,128)(2,1)} %param.11), kind=kLoop, calls=%fused_computation.29 | loop fusion | flops 28311552 | bytes 19170304 | tf_op jit(solution)/shard_map/convert_element_type | solution.py:60
  48.3 0.0 all-gather.2.cloned.1.call-update
  48.3 0.0 reduce-scatter.2.cloned.1.call-start
  48.4 0.1 fusion.48
  48.5 0.5 convolution_select_fusion.1
  49.0 28.7 %fusion.34 = f32[192,192,256]{2,1,0:T(8,128)} fusion(bf16[128,256]{1,0:T(8,128)(2,1)S(1)} %copy-done.2, bf16[192,192,128]{2,0,1:T(8,128)(2,1)} %fusion.20), kind=kOutput, calls=%fused_computation.51 | convolution fusion | flops 2415919104 | bytes 47251456 | tf_op jit(solution)/shard_map/dot_general | solution.py:18
  77.6 20.0 %fusion.21 = bf16[192,192,128]{2,1,0:T(8,128)(2,1)} fusion(f32[192,192,256]{2,1,0:T(8,128)} %fusion.34, f32[192,192]{1,0:T(8,128)S(1)} %convolution_select_fusion.1), kind=kLoop, calls=%fused_computation.31 | loop fusion | flops 28311552 | bytes 47333376 | tf_op jit(solution)/shard_map/convert_element_type | solution.py:20
  97.7 17.4 %copy.25 = bf16[192,192,128]{1,0,2:T(8,128)(2,1)} copy(bf16[192,192,128]{2,1,0:T(8,128)(2,1)} %fusion.21) | data formatting | bytes 18874368 | tf_op jit(solution)/shard_map/convert_element_type | solution.py:20
  115.1 0.5 convolution_select_fusion
  115.5 562.9 %all-gather.2.cloned.1.call-done = bf16[768,192,128]{2,0,1:T(8,128)(2,1)} async-done(((bf16[192,192,128]{2,0,1:T(8,128)(2,1)}), bf16[768,192,128]{2,0,1:T(8,128)(2,1)}) %all-gather.2.cloned.1.call-update) | async-done | bytes 37748752 | tf_op jit(solution)/shard_map/all_gather | solution.py:63
  678.5 63.8 %fusion.32 = f32[768,192,256]{2,0,1:T(8,128)} fusion(bf16[768,192,128]{2,0,1:T(8,128)(2,1)} %all-gather.2.cloned.1.call-done, bf16[128,256]{1,0:T(8,128)(2,1)S(1)} %copy-done), kind=kOutput, calls=%fused_computation.49 | convolution fusion | flops 9663676416 | bytes 188809216 | tf_op jit(solution)/shard_map/dot_general | solution.py:18
  742.3 59.9 %fusion = bf16[768,192,128]{2,0,1:T(8,128)(2,1)} fusion(f32[768,192,256]{2,0,1:T(8,128)} %fusion.32, f32[768,192]{0,1:T(8,128)S(1)} %convolution_select_fusion), kind=kLoop, calls=%fused_computation.1 | loop fusion | flops 113246208 | bytes 189333504 | tf_op jit(solution)/shard_map/convert_element_type | solution.py:20
  802.2 47.5 %copy.26 = bf16[768,192,128]{0,1,2:T(8,128)(2,1)} copy(bf16[768,192,128]{2,0,1:T(8,128)(2,1)} %fusion) | data formatting | bytes 75497472 | tf_op jit(solution)/shard_map/convert_element_type | solution.py:20
  849.7 33.3 %convert_bitcast_fusion = bf16[768,192,128]{0,1,2:T(8,128)(2,1)} fusion(bf16[192,192,128]{1,0,2:T(8,128)(2,1)} %copy.25, bf16[768,192,128]{0,1,2:T(8,128)(2,1)} %copy.26), kind=kOutput, calls=%fused_computation.13 | convolution fusion | flops 7266631680 | bytes 84934656 | tf_op jit(solution)/shard_map/jkh,ikh->jih/dot_general | solution.py:69
  883.0 52.4 %copy.27 = bf16[768,192,128]{2,1,0:T(8,128)(2,1)} copy(bf16[768,192,128]{0,1,2:T(8,128)(2,1)} %convert_bitcast_fusion) | data formatting | bytes 75497472 | tf_op jit(solution)/shard_map/convert_element_type | solution.py:69
  935.4 0.0 reduce-scatter.2.cloned.1.call-update
  935.4 0.0 copy-start.10
  935.4 15.4 %copy.23 = bf16[192,192,128]{2,1,0:T(8,128)(2,1)} copy(bf16[192,192,128]{2,0,1:T(8,128)(2,1)} %fusion.20) | data formatting | bytes 18874368 | tf_op jit(solution)/shard_map/convert_element_type | solution.py:60
  950.8 17.1 %fusion.8 = f32[36864,128]{1,0:T(8,128)} fusion(bf16[36864,128]{1,0:T(8,128)(2,1)} %bitcast.21, bf16[128,128]{1,0:T(8,128)(2,1)S(1)} %copy-done.10), kind=kOutput, calls=%fused_computation.12 | convolution fusion | flops 1222115328 | bytes 28344320 | tf_op jit(solution)/shard_map/dot_general | solution.py:78
  967.9 0.0 copy-start.8
  967.9 0.0 copy-start.9
  968.0 0.0 copy-start.3
  968.0 230.4 %reduce-scatter.2.cloned.1.call-done = bf16[192,192,128]{2,1,0:T(8,128)(2,1)} async-done(((bf16[768,192,128]{2,1,0:T(8,128)(2,1)}), bf16[192,192,128]{2,1,0:T(8,128)(2,1)}) %reduce-scatter.2.cloned.1.call-update) | async-done | bytes 9437200 | tf_op jit(solution)/shard_map/reduce_scatter | solution.py:68
  1198.3 13.9 %convert_reduce_fusion = f32[192,192]{0,1:T(8,128)S(1)} fusion(bf16[192,192,128]{2,1,0:T(8,128)(2,1)} %reduce-scatter.2.cloned.1.call-done), kind=kLoop, calls=%fused_computation.15 | loop fusion | flops 9400320 | bytes 9584640 | tf_op jit(solution)/shard_map/reduce_sum | solution.py:10
  1212.3 14.0 %fusion.13 = f32[192,192]{0,1:T(8,128)S(1)} fusion(f32[192,192]{0,1:T(8,128)S(1)} %broadcast_multiply_fusion, bf16[192,192,128]{2,1,0:T(8,128)(2,1)} %reduce-scatter.2.cloned.1.call-done), kind=kLoop, calls=%fused_computation.22 | loop fusion | flops 18837504 | bytes 9732096 | tf_op jit(solution)/shard_map/reduce_sum | solution.py:12
  1226.3 13.7 %fusion.16 = bf16[192,192,128]{2,0,1:T(8,128)(2,1)} fusion(f32[128]{0:T(128)S(1)} %copy-done.8, f32[128]{0:T(128)S(1)} %copy-done.9, f32[192,192]{0,1:T(8,128)S(1)} %add_rsqrt_fusion, f32[192,192]{0,1:T(8,128)S(1)} %broadcast_multiply_fusion, bf16[192,192,128]{2,1,0:T(8,128)(2,1)} %reduce-scatter.2.cloned.1.call-done), kind=kLoop, calls=%fused_computation.25 | loop fusion | flops 28311552 | bytes 19170304 | tf_op jit(solution)/shard_map/convert_element_type | solution.py:76
  1240.0 14.4 %fusion.7 = bf16[36864,128]{1,0:T(8,128)(2,1)} fusion(f32[36864,128]{1,0:T(8,128)} %fusion.8, bf16[36864,128]{1,0:T(8,128)(2,1)} %bitcast.20, bf16[128,128]{1,0:T(8,128)(2,1)S(1)} %copy-done.3), kind=kOutput, calls=%fused_computation.11 | convolution fusion | flops 1217396736 | bytes 37781504 | tf_op jit(solution)/shard_map/dot_general | solution.py:80
  (22 shorter events, 0.1 us)
Async XLA Ops:
  6.5 671.9 %copy-start = (bf16[128,256]{1,0:T(8,128)(2,1)S(1)}, bf16[128,256]{1,0:T(8,128)(2,1)}, u32[]{:S(2)}) copy-start(bf16[128,256]{1,0:T(8,128)(2,1)} %param.17) | copy-start | bytes 196612
  6.5 28.1 %copy-start.7 = (f32[128]{0:T(128)S(1)}, f32[128]{0:T(128)}, u32[]{:S(2)}) copy-start(f32[128]{0:T(128)} %param.14) | copy-start | bytes 1540
  6.5 28.1 %copy-start.6 = (f32[128]{0:T(128)S(1)}, f32[128]{0:T(128)}, u32[]{:S(2)}) copy-start(f32[128]{0:T(128)} %param.15) | copy-start | bytes 1540
  6.5 671.9 %all-gather.2.cloned.1.call-start = ((), (), s32[]{:S(2)}) async-start(), calls=%async_computation.1 | async-start | bytes 47185920 | tf_op jit(solution)/shard_map/all_gather | solution.py:63
  20.5 27.9 %copy-start.4 = (s32[768]{0:T(1024)S(1)}, s32[768]{0:T(1024)}, u32[]{:S(2)}) copy-start(s32[768]{0:T(1024)} %param.12) | copy-start | bytes 9220
  20.5 28.0 %copy-start.5 = (s32[6,6]{1,0:T(8,128)S(1)}, s32[6,6]{1,0:T(8,128)}, u32[]{:S(2)}) copy-start(s32[6,6]{1,0:T(8,128)} %param.13) | copy-start | bytes 436
  20.5 28.5 %copy-start.2 = (bf16[128,256]{1,0:T(8,128)(2,1)S(1)}, bf16[128,256]{1,0:T(8,128)(2,1)}, u32[]{:S(2)}) copy-start(bf16[128,256]{1,0:T(8,128)(2,1)} %param.16) | copy-start | bytes 196612
  48.3 1150.0 %reduce-scatter.2.cloned.1.call-start = ((), (), s32[]{:S(2)}) async-start(), calls=%async_computation.2 | async-start | bytes 47185920 | tf_op jit(solution)/shard_map/reduce_scatter | solution.py:68
  935.4 15.4 %copy-start.10 = (bf16[128,128]{1,0:T(8,128)(2,1)S(1)}, bf16[128,128]{1,0:T(8,128)(2,1)}, u32[]{:S(2)}) copy-start(bf16[128,128]{1,0:T(8,128)(2,1)} %param.18) | copy-start | bytes 98308
  967.9 258.4 %copy-start.8 = (f32[128]{0:T(128)S(1)}, f32[128]{0:T(128)}, u32[]{:S(2)}) copy-start(f32[128]{0:T(128)} %param.20) | copy-start | bytes 1540
  967.9 258.4 %copy-start.9 = (f32[128]{0:T(128)S(1)}, f32[128]{0:T(128)}, u32[]{:S(2)}) copy-start(f32[128]{0:T(128)} %param.19) | copy-start | bytes 1540
  968.0 272.1 %copy-start.3 = (bf16[128,128]{1,0:T(8,128)(2,1)S(1)}, bf16[128,128]{1,0:T(8,128)(2,1)}, u32[]{:S(2)}) copy-start(bf16[128,128]{1,0:T(8,128)(2,1)} %param.21) | copy-start | bytes 98308
  1240.0 14.5 %copy-start.1 = (bf16[128,256]{1,0:T(8,128)(2,1)S(1)}, bf16[128,256]{1,0:T(8,128)(2,1)}, u32[]{:S(2)}) copy-start(bf16[128,256]{1,0:T(8,128)(2,1)} %param.17) | copy-start | bytes 196612
Sparse Core Ops, SparseCore 0:
  48.5 629.9 all-gather.1
  935.5 262.7 reduce-scatter.1
where the time goes:
time: 1280 us; the launch traced here: 1260 us
  waiting for transfers between devices  793 us (62%)
  other arithmetic  163 us (13%)
  matrix products  158 us (12%)
  local copies, waits for them, and re-layouts  133 us (10%)
  between operations  14 us (1%)
    all_gather x1, waiting for transfers between devices, shards(): piece = lax.all_gather(normed, 'col', axis=0, tiled=True)  563 us
    reduce_scatter x1, waiting for transfers between devices, shards(): lax.psum_scatter(jnp.einsum('jkh,ikh->jih', right_all, left, preferred_el...  230 us
    dot_general x2, matrix products, gated_projection(): jnp.dot(normed.reshape(-1, normed.shape[-1]), weight, preferred_element_t...  92.4 us
    convert_element_type x2, other arithmetic, gated_projection(): (mask[..., None] * jax.nn.sigmoid(both[..., hidden:]) * both[..., :hidden...  79.9 us
    convert_element_type x2, local copies, waits for them, and re-layouts, gated_projection(): (mask[..., None] * jax.nn.sigmoid(both[..., hidden:]) * both[..., :hidden...  64.9 us
    convert_element_type x1, local copies, waits for them, and re-layouts, shards(): jnp.einsum('jkh,ikh->jih', right_all, left, preferred_element_type=jnp.fl...  52.4 us
    dot_general x1, matrix products, shards(): jnp.einsum('jkh,ikh->jih', right_all, left, preferred_element_type=jnp.fl...  33.3 us
    reduce_sum x2, other arithmetic, layer_norm(): spread = jnp.mean(centered * centered, axis=-1, keepdims=True)  28 us
  transfers between devices with their start and end apart: 2, of which 2 were waited for; matrix products, arithmetic and copies ran while one was open for 8% of the time, Pallas kernels for 0%

commit v1 on v0

--- a/solution.py
+++ b/solution.py
@@ -83,6 +83,129 @@
     return (gate * projected).reshape(tile_rows, tile_cols, channels).astype(jnp.bfloat16)
 
 
+NEIGHBOUR = ((0, 1), (1, 0), (2, 3), (3, 2))
+MIDDLE = ((1, 2), (2, 1))
+CORE_PAIRS = ((0, 1), (1, 0), (2, 3), (3, 2))
+CHIP_PAIRS = ((0, 2), (2, 0), (1, 3), (3, 1))
+FIRST_BLOCK = (0, 2, 1, 3)
+SECOND_BLOCK = (1, 3, 0, 2)
+OTHER_BLOCK = (1, 0, 3, 2)
+CHUNKS = 4
+
+
+def pick(table, index):
+    result = jnp.int32(table[0])
+    for position in range(1, len(table)):
+        result = jnp.where(index == position, jnp.int32(table[position]), result)
+    return result
+
+
+def owners():
+    moves = []
+    for layer in range(4):
+        for slot in range(4):
+            i_block = (layer, OTHER_BLOCK[layer])[slot // 2]
+            j_block = (FIRST_BLOCK[layer], SECOND_BLOCK[layer])[slot % 2]
+            moves.append((slot * 4 + layer, j_block * 4 + i_block))
+    return tuple(move for move in moves if move[0] != move[1])
+
+
+def sum_over_row(partial, place):
+    core, chip = place % 2, place // 2
+    kept = lax.dynamic_index_in_dim(partial, core, 1, keepdims=False)
+    sent = lax.dynamic_index_in_dim(partial, 1 - core, 1, keepdims=False)
+    came = lax.ppermute(sent, "row", CORE_PAIRS)
+    pairs = (kept.astype(jnp.float32) + came.astype(jnp.float32)).astype(jnp.bfloat16)
+    kept = lax.dynamic_index_in_dim(pairs, chip, 0, keepdims=False)
+    sent = lax.dynamic_index_in_dim(pairs, 1 - chip, 0, keepdims=False)
+    came = lax.ppermute(sent, "row", CHIP_PAIRS)
+    return (kept.astype(jnp.float32) + came.astype(jnp.float32)).astype(jnp.bfloat16)
+
+
+def blocked(
+    pair,
+    chain_ids,
+    block_keep,
+    norm_gain,
+    norm_bias,
+    left_weight,
+    right_weight,
+    gate_weight,
+    out_gain,
+    out_bias,
+    out_weight,
+):
+    tile_rows, tile_cols, channels = pair.shape
+    hidden = left_weight.shape[1] // 2
+    depth = tile_rows // CHUNKS
+    layer = lax.axis_index("col")
+    place = lax.axis_index("row")
+    col_start = place * tile_cols
+    keep_table = block_keep.astype(jnp.float32)
+    at_end = (layer == 0) | (layer == 3)
+    stays = jnp.bool_(False)
+    moved_from = [move[0] for move in owners()]
+    for spot in range(16):
+        if spot not in moved_from:
+            stays = stays | (place * 4 + layer == spot)
+
+    def mask_of(block, chunk):
+        start = block * tile_rows + chunk * depth
+        return pair_mask(chain_ids, keep_table, start, depth, col_start, tile_cols)
+
+    own, other, first, second = [], [], [], []
+    for chunk in range(CHUNKS):
+        piece = pair[chunk * depth : (chunk + 1) * depth]
+        own.append(layer_norm(piece.astype(jnp.float32), norm_gain, norm_bias).astype(jnp.bfloat16))
+        other.append(lax.ppermute(own[chunk], "col", NEIGHBOUR))
+        first.append(jnp.where(at_end, own[chunk], lax.ppermute(own[chunk], "col", MIDDLE)))
+        second.append(jnp.where(at_end, other[chunk], lax.ppermute(other[chunk], "col", MIDDLE)))
+
+    left = []
+    for block, pieces in ((layer, own), (pick(OTHER_BLOCK, layer), other)):
+        parts = [
+            gated_projection(pieces[chunk], left_weight, mask_of(block, chunk))
+            for chunk in range(CHUNKS)
+        ]
+        left.append(jnp.concatenate(parts, axis=0))
+    left = jnp.stack(left)
+
+    gate_in = jnp.concatenate(own, axis=0)
+    results = []
+    for chunk in range(CHUNKS):
+        right = jnp.stack(
+            [
+                gated_projection(
+                    pieces[chunk], right_weight, mask_of(pick(table, layer), chunk)
+                )
+                for table, pieces in ((FIRST_BLOCK, first), (SECOND_BLOCK, second))
+            ]
+        )
+        partial = jnp.einsum(
+            "pjkh,qikh->qpjih", right, left, preferred_element_type=jnp.float32
+        ).astype(jnp.bfloat16)
+        summed = sum_over_row(partial, place)
+        moved = lax.ppermute(summed, ("row", "col"), owners())
+        summed = jnp.where(stays, summed, moved).astype(jnp.float32)
+        out_normed = jnp.swapaxes(
+            layer_norm(summed, out_gain, out_bias).astype(jnp.bfloat16), 0, 1
+        )
+        gate = jax.nn.sigmoid(
+            jnp.dot(
+                gate_in[:, chunk * depth : (chunk + 1) * depth].reshape(-1, channels),
+                gate_weight,
+                preferred_element_type=jnp.float32,
+            )
+        )
+        projected = jnp.dot(
+            out_normed.reshape(-1, hidden), out_weight, preferred_element_type=jnp.float32
+        )
+        results.append(
+            (gate * projected).reshape(tile_rows, depth, channels).astype(jnp.bfloat16)
+        )
+    return jnp.concatenate(results, axis=1)
+
+
 def solution(mesh):
     placed = (
         P(("crop", "col"), "row", None),
@@ -98,7 +221,7 @@
         P(),
     )
     return jax.shard_map(
-        shards,
+        blocked if (mesh.shape["col"], mesh.shape["row"]) == (4, 4) else shards,
         mesh=mesh,
         in_specs=placed,
         out_specs=P(("crop", "col"), "row", None),

time: 1280 us -> 1080 us (0.84); the launches traced: 1260 us -> 1080 us
  waiting for transfers between devices: 793 us -> 340 us
  local copies, waits for them, and re-layouts: 133 us -> 322 us
  starting transfers between devices: 0.04 us -> 43.2 us
  other arithmetic: 163 us -> 191 us
  matrix products: 158 us -> 177 us
    all_gather x1 -> x0, waiting for transfers between devices: 563 us -> none  [shards(): piece = lax.all_gather(normed, 'col', axis=0, tiled=True)]
    ppermute x0 -> x24, waiting for transfers between devices: none -> 340 us  [the longest x4 212 us: sum_over_row(): came = lax.ppermute(sent, 'row', CHIP_PAIRS)]
    reduce_scatter x1 -> x0, waiting for transfers between devices: 230 us -> none  [shards(): lax.psum_scatter(jnp.einsum('jkh,ikh->jih', right_all, left, preferred_el...]
    convert_element_type x4, local copies, waits for them, and re-layouts: 133 us -> 15.8 us  [sum_over_row(): (kept.astype(jnp.float32) + came.astype(jnp.float32)).astype(jnp.bfloat16)]
    another operation x0 -> x6, local copies, waits for them, and re-layouts: none -> 104 us  [the longest x2 68.3 us: blocked(): left = jnp.stack(left)]
    ppermute x0 -> x12, local copies, waits for them, and re-layouts: none -> 75.9 us  [the longest x4 36.2 us: sum_over_row(): came = lax.ppermute(sent, 'row', CORE_PAIRS)]
    squeeze x0 -> x8, local copies, waits for them, and re-layouts: none -> 58.9 us  [sum_over_row(): sent = lax.dynamic_index_in_dim(partial, 1 - core, 1, keepdims=False)]
    convert_element_type x2 -> x8, other arithmetic: 79.9 us -> 31.9 us  [gated_projection(): (mask[..., None] * jax.nn.sigmoid(both[..., hidden:]) * both[..., :hidden...]
  transfers between devices with their start and end apart: 2 -> 24, of which waited for: 2 -> 7; matrix products, arithmetic and copies ran while one was open for 8% -> 55% of each run, Pallas kernels for 0% -> 0%
where the time goes in v1:
time: 1080 us
  waiting for transfers between devices  340 us (31%)
  local copies, waits for them, and re-layouts  322 us (30%)
  other arithmetic  191 us (18%)
  matrix products  177 us (16%)
  starting transfers between devices  43.2 us (4%)
    ppermute x4, waiting for transfers between devices, sum_over_row(): came = lax.ppermute(sent, 'row', CHIP_PAIRS)  212 us
    ppermute x4, waiting for transfers between devices, blocked(): other.append(lax.ppermute(own[chunk], 'col', NEIGHBOUR))  106 us
    dot_general x4, matrix products, blocked(): jnp.einsum('pjkh,qikh->qpjih', right, left, preferred_element_type=jnp.fl...  75.5 us
    another operation x2, local copies, waits for them, and re-layouts, blocked(): left = jnp.stack(left)  68.3 us
    dot_general x16, matrix products, gated_projection(): jnp.dot(normed.reshape(-1, normed.shape[-1]), weight, preferred_element_t...  65.4 us
    squeeze x8, local copies, waits for them, and re-layouts, sum_over_row(): sent = lax.dynamic_index_in_dim(partial, 1 - core, 1, keepdims=False)  58.9 us
    convert_element_type x8, other arithmetic, sum_over_row(): (kept.astype(jnp.float32) + came.astype(jnp.float32)).astype(jnp.bfloat16)  43.3 us
    ppermute x4, local copies, waits for them, and re-layouts, sum_over_row(): came = lax.ppermute(sent, 'row', CORE_PAIRS)  36.2 us
  transfers between devices with their start and end apart: 24, of which 7 were waited for; matrix products, arithmetic and copies ran while one was open for 55% of the time, Pallas kernels for 0%

profile of v1, /device:TPU:8, one launch (start us, length us, event | category | flops | bytes accessed | tf_op | source)
XLA Modules:
  0.0 1075.4 jit_solution(7121483149695491288)
XLA Ops:
  6.5 12.9 %fusion.68 = (f32[48,192]{1,0:T(8,128)S(1)}, f32[48,192]{1,0:T(8,128)S(1)}, f32[48,192]{1,0:T(8,128)S(1)}, f32[48,192]{1,0:T(8,128)S(1)}) fusion(f32[48,192]{1,0:T(8,128)S(1)} %get-tuple-element.56, bf16[192,192,128]{2,1,0:T(8,128)(2,1)S(1)} %copy-done.2, f32[48,192]{1,0:T(8,128)S(1)} %get-tuple-element.55, f32[48,192]{1,0:T(8,128)S(1)} %get-tuple-element.54, ...), kind=kLoop, calls=%fused_computation.113 | loop fusion | flops 18837504 | bytes 9732096 | tf_op jit(solution)/shard_map/reduce_sum | solution.py:12
  19.5 12.7 %fusion.71 = (bf16[48,192,128]{2,1,0:T(8,128)(2,1)S(1)}, bf16[48,192,128]{2,1,0:T(8,128)(2,1)}, bf16[48,192,128]{2,1,0:T(8,128)(2,1)}, bf16[48,192,128]{2,1,0:T(8,128)(2,1)}) fusion(f32[128]{0:T(128)S(1)} %copy-done.33, f32[128]{0:T(128)S(1)} %copy-done.34, f32[48,192]{1,0:T(8,128)S(1)} %add_rsqrt_fusion.7, f32[48,192]{1,0:T(8,128)S(1)} %get-tuple-element.56, ...), kind=kLoop, calls=%fused_computation.116 | loop fusion | flops 28311552 | bytes 19170304 | tf_op jit(solution)/shard_map/convert_element_type | solution.py:159
  95.2 9.4 maximum_bitcast_fusion.1
  114.8 22.5 %collective-permute-done.2 = bf16[48,192,128]{2,1,0:T(8,128)(2,1)} collective-permute-done((bf16[48,192,128]{2,1,0:T(8,128)(2,1)}, bf16[48,192,128]{2,1,0:T(8,128)(2,1)}, u32[]{:S(2)}, u32[]{:S(2)}) %collective-permute-start.2) | collective-permute-done | bytes 2359328 | tf_op jit(solution)/shard_map/ppermute | solution.py:160
  144.2 43.6 %collective-permute-done.1 = bf16[48,192,128]{2,1,0:T(8,128)(2,1)} collective-permute-done((bf16[48,192,128]{2,1,0:T(8,128)(2,1)}, bf16[48,192,128]{2,1,0:T(8,128)(2,1)}, u32[]{:S(2)}, u32[]{:S(2)}) %collective-permute-start.1) | collective-permute-done | bytes 2359328 | tf_op jit(solution)/shard_map/ppermute | solution.py:160
  197.7 39.5 %collective-permute-done = bf16[48,192,128]{2,1,0:T(8,128)(2,1)} collective-permute-done((bf16[48,192,128]{2,1,0:T(8,128)(2,1)S(1)}, bf16[48,192,128]{2,1,0:T(8,128)(2,1)}, u32[]{:S(2)}, u32[]{:S(2)}) %collective-permute-start) | collective-permute-done | bytes 2359328 | tf_op jit(solution)/shard_map/ppermute | solution.py:160
  244.3 8.0 maximum_bitcast_fusion
  252.4 34.1 %copy.114 = bf16[2,192,192,128,1]{2,1,4,0,3:T(8,128)(2,1)} copy(bf16[2,192,192,128,1]{3,2,1,0,4:T(8,128)(2,1)} %maximum_bitcast_fusion) | data formatting | bytes 37748736 | tf_op jit(solution)/shard_map/stack | solution.py:171
  310.1 6.8 fusion.166
  316.9 34.2 %copy.116 = bf16[2,192,192,128,1]{2,1,3,0,4:T(8,128)(2,1)} copy(bf16[2,192,192,128,1]{3,2,1,0,4:T(8,128)(2,1)} %maximum_bitcast_fusion) | data formatting | bytes 37748736 | tf_op jit(solution)/shard_map/stack | solution.py:171
  367.5 9.0 copy.123
  376.5 18.9 %convolution_convert_fusion = bf16[128,2,192,2,48]{2,4,0,1,3:T(8,128)(2,1)} fusion(bf16[2,192,192,128,1]{2,1,3,0,4:T(8,128)(2,1)} %copy.116, bf16[2,48,192,128,1]{2,1,3,4,0:T(8,128)(2,1)} %copy.123), kind=kOutput, calls=%fused_computation.53 | convolution fusion | flops 1816657920 | bytes 33030144 | tf_op jit(solution)/shard_map/pjkh,qikh->qpjih/dot_general | solution.py:184
  401.3 8.8 copy.107
  417.4 9.0 copy.120
  426.4 18.9 %convolution_convert_fusion.1 = bf16[128,2,192,2,48]{2,4,0,1,3:T(8,128)(2,1)} fusion(bf16[2,192,192,128,1]{2,1,3,0,4:T(8,128)(2,1)} %copy.116, bf16[2,48,192,128,1]{2,1,3,4,0:T(8,128)(2,1)} %copy.120), kind=kOutput, calls=%fused_computation.54 | convolution fusion | flops 1816657920 | bytes 33030144 | tf_op jit(solution)/shard_map/pjkh,qikh->qpjih/dot_general | solution.py:184
  451.1 8.9 copy.97
  467.9 9.0 copy.117
  476.9 18.9 %convolution_convert_fusion.2 = bf16[128,2,192,2,48]{2,4,0,1,3:T(8,128)(2,1)} fusion(bf16[2,192,192,128,1]{2,1,3,0,4:T(8,128)(2,1)} %copy.116, bf16[2,48,192,128,1]{2,1,3,4,0:T(8,128)(2,1)} %copy.117), kind=kOutput, calls=%fused_computation.55 | convolution fusion | flops 1816657920 | bytes 33030144 | tf_op jit(solution)/shard_map/pjkh,qikh->qpjih/dot_general | solution.py:184
  501.6 8.8 copy.87
  517.8 9.0 copy.115
  526.8 18.9 %convolution_convert_fusion.3 = bf16[128,2,192,2,48]{2,4,3,1,0:T(8,128)(2,1)} fusion(bf16[2,192,192,128,1]{2,1,4,0,3:T(8,128)(2,1)} %copy.114, bf16[2,48,192,128,1]{2,1,0,4,3:T(8,128)(2,1)} %copy.115), kind=kOutput, calls=%fused_computation.56 | convolution fusion | flops 1816657920 | bytes 33030144 | tf_op jit(solution)/shard_map/pjkh,qikh->qpjih/dot_general | solution.py:184
  551.6 8.8 copy.77
  571.0 9.0 copy.108
  597.4 9.0 copy.98
  626.3 9.0 copy.88
  652.6 9.1 copy.78
  661.7 7.4 fusion.3
  694.7 56.7 %collective-permute-done.17 = bf16[48,192,128]{2,1,0:T(8,128)(2,1)} collective-permute-done((bf16[48,192,128]{2,1,0:T(8,128)(2,1)}, bf16[48,192,128]{2,1,0:T(8,128)(2,1)}, u32[]{:S(2)}, u32[]{:S(2)}) %collective-permute-start.17) | collective-permute-done | bytes 2359328 | tf_op jit(solution)/shard_map/ppermute | solution.py:121
  777.5 75.0 %collective-permute-done.12 = bf16[48,192,128]{2,1,0:T(8,128)(2,1)} collective-permute-done((bf16[48,192,128]{2,1,0:T(8,128)(2,1)}, bf16[48,192,128]{2,1,0:T(8,128)(2,1)}, u32[]{:S(2)}, u32[]{:S(2)}) %collective-permute-start.12) | collective-permute-done | bytes 2359328 | tf_op jit(solution)/shard_map/ppermute | solution.py:121
  872.0 80.7 %collective-permute-done.7 = bf16[48,192,128]{2,1,0:T(8,128)(2,1)} collective-permute-done((bf16[48,192,128]{2,1,0:T(8,128)(2,1)}, bf16[48,192,128]{2,1,0:T(8,128)(2,1)}, u32[]{:S(2)}, u32[]{:S(2)}) %collective-permute-start.7) | collective-permute-done | bytes 2359328 | tf_op jit(solution)/shard_map/ppermute | solution.py:121
  998.2 22.2 %collective-permute-done.8 = bf16[48,192,128]{2,1,0:T(8,128)(2,1)} collective-permute-done((bf16[48,192,128]{2,1,0:T(8,128)(2,1)}, bf16[48,192,128]{2,1,0:T(8,128)(2,1)}, u32[]{:S(2)}, u32[]{:S(2)}) %collective-permute-start.8) | collective-permute-done | bytes 2359328 | tf_op jit(solution)/shard_map/ppermute | solution.py:188
  1029.5 9.0 fusion.152
  (269 shorter events, 416.1 us)
Async XLA Ops:
  0.0 39.8 %copy-start = (bf16[128,256]{1,0:T(8,128)(2,1)S(1)}, bf16[128,256]{1,0:T(8,128)(2,1)}, u32[]{:S(2)}) copy-start(bf16[128,256]{1,0:T(8,128)(2,1)} %param.16) | copy-start | bytes 196612
  6.5 13.0 %copy-start.33 = (f32[128]{0:T(128)S(1)}, f32[128]{0:T(128)}, u32[]{:S(2)}) copy-start(f32[128]{0:T(128)} %param.15) | copy-start | bytes 1540
  6.5 13.0 %copy-start.34 = (f32[128]{0:T(128)S(1)}, f32[128]{0:T(128)}, u32[]{:S(2)}) copy-start(f32[128]{0:T(128)} %param.14) | copy-start | bytes 1540
  32.2 319.0 %copy-start.3 = (bf16[48,192,128]{2,1,0:T(8,128)(2,1)}, bf16[48,192,128]{2,1,0:T(8,128)(2,1)S(1)}, u32[]{:S(2)}) copy-start(bf16[48,192,128]{2,1,0:T(8,128)(2,1)S(1)} %get-tuple-element.21) | copy-start | bytes 7077892
  32.2 75.4 %collective-permute-start.3 = (bf16[48,192,128]{2,1,0:T(8,128)(2,1)}, bf16[48,192,128]{2,1,0:T(8,128)(2,1)}, u32[]{:S(2)}, u32[]{:S(2)}) collective-permute-start(bf16[48,192,128]{2,1,0:T(8,128)(2,1)} %get-tuple-element.24), channel_id=1, source_target_pairs={{0,1},{1,0},{2,3},{3,2},{4,5},{5,4},{6,7},{7,6},{8,9},{9,8},{10,11... | collective-permute-start | bytes 7077896 | tf_op jit(solution)/shard_map/ppermute | solution.py:160
  32.2 257.7 %collective-permute-start.19 = (bf16[48,192,128]{2,1,0:T(8,128)(2,1)}, bf16[48,192,128]{2,1,0:T(8,128)(2,1)}, u32[]{:S(2)}, u32[]{:S(2)}) collective-permute-start(bf16[48,192,128]{2,1,0:T(8,128)(2,1)} %get-tuple-element.24), channel_id=1, source_target_pairs={{1,2},{2,1},{5,6},{6,5},{9,10},{10,9},{13,14},{14,13},{17,18},{18,... | collective-permute-start | bytes 7077896 | tf_op jit(solution)/shard_map/ppermute | solution.py:161
  37.5 99.7 %collective-permute-start.2 = (bf16[48,192,128]{2,1,0:T(8,128)(2,1)}, bf16[48,192,128]{2,1,0:T(8,128)(2,1)}, u32[]{:S(2)}, u32[]{:S(2)}) collective-permute-start(bf16[48,192,128]{2,1,0:T(8,128)(2,1)} %get-tuple-element.23), channel_id=1, source_target_pairs={{0,1},{1,0},{2,3},{3,2},{4,5},{5,4},{6,7},{7,6},{8,9},{9,8},{10,11... | collective-permute-start | bytes 7077896 | tf_op jit(solution)/shard_map/ppermute | solution.py:160
  37.6 150.2 %collective-permute-start.1 = (bf16[48,192,128]{2,1,0:T(8,128)(2,1)}, bf16[48,192,128]{2,1,0:T(8,128)(2,1)}, u32[]{:S(2)}, u32[]{:S(2)}) collective-permute-start(bf16[48,192,128]{2,1,0:T(8,128)(2,1)} %get-tuple-element.22), channel_id=1, source_target_pairs={{0,1},{1,0},{2,3},{3,2},{4,5},{5,4},{6,7},{7,6},{8,9},{9,8},{10,11... | collective-permute-start | bytes 7077896 | tf_op jit(solution)/shard_map/ppermute | solution.py:160
  39.6 197.6 %collective-permute-start = (bf16[48,192,128]{2,1,0:T(8,128)(2,1)S(1)}, bf16[48,192,128]{2,1,0:T(8,128)(2,1)}, u32[]{:S(2)}, u32[]{:S(2)}) collective-permute-start(bf16[48,192,128]{2,1,0:T(8,128)(2,1)S(1)} %get-tuple-element.21), channel_id=1, source_target_pairs={{0,1},{1,0},{2,3},{3,2},{4,5},{5,4},{6,7},{7,6},{8,9},{9,8},{10,11... | collective-permute-start | bytes 7077896 | tf_op jit(solution)/shard_map/ppermute | solution.py:160
  107.5 187.9 %collective-permute-start.14 = (bf16[48,192,128]{2,1,0:T(8,128)(2,1)}, bf16[48,192,128]{2,1,0:T(8,128)(2,1)}, u32[]{:S(2)}, u32[]{:S(2)}) collective-permute-start(bf16[48,192,128]{2,1,0:T(8,128)(2,1)} %get-tuple-element.23), channel_id=1, source_target_pairs={{1,2},{2,1},{5,6},{6,5},{9,10},{10,9},{13,14},{14,13},{17,18},{18,... | collective-permute-start | bytes 7077896 | tf_op jit(solution)/shard_map/ppermute | solution.py:161
  137.2 170.5 %collective-permute-start.9 = (bf16[48,192,128]{2,1,0:T(8,128)(2,1)}, bf16[48,192,128]{2,1,0:T(8,128)(2,1)}, u32[]{:S(2)}, u32[]{:S(2)}) collective-permute-start(bf16[48,192,128]{2,1,0:T(8,128)(2,1)} %get-tuple-element.22), channel_id=1, source_target_pairs={{1,2},{2,1},{5,6},{6,5},{9,10},{10,9},{13,14},{14,13},{17,18},{18,... | collective-permute-start | bytes 7077896 | tf_op jit(solution)/shard_map/ppermute | solution.py:161
  187.8 163.3 %collective-permute-start.4 = (bf16[48,192,128]{2,1,0:T(8,128)(2,1)S(1)}, bf16[48,192,128]{2,1,0:T(8,128)(2,1)}, u32[]{:S(2)}, u32[]{:S(2)}) collective-permute-start(bf16[48,192,128]{2,1,0:T(8,128)(2,1)S(1)} %get-tuple-element.21), channel_id=1, source_target_pairs={{1,2},{2,1},{5,6},{6,5},{9,10},{10,9},{13,14},{14,13},{17,18},{18,... | collective-permute-start | bytes 7077896 | tf_op jit(solution)/shard_map/ppermute | solution.py:161
  252.4 40.0 %copy-start.26 = (bf16[128,256]{1,0:T(8,128)(2,1)S(1)}, bf16[128,256]{1,0:T(8,128)(2,1)}, u32[]{:S(2)}) copy-start(bf16[128,256]{1,0:T(8,128)(2,1)} %param.17) | copy-start | bytes 196612
  286.5 73.6 %collective-permute-start.20 = (bf16[48,192,128]{2,1,0:T(8,128)(2,1)}, bf16[48,192,128]{2,1,0:T(8,128)(2,1)}, u32[]{:S(2)}, u32[]{:S(2)}) collective-permute-start(bf16[48,192,128]{2,1,0:T(8,128)(2,1)} %collective-permute-done.3), channel_id=1, source_target_pairs={{1,2},{2,1},{5,6},{6,5},{9,10},{10,9},{13,14},{14,13},{17,18},{18,... | collective-permute-start | bytes 7077896 | tf_op jit(solution)/shard_map/ppermute | solution.py:162
  290.0 120.1 %collective-permute-start.15 = (bf16[48,192,128]{2,1,0:T(8,128)(2,1)}, bf16[48,192,128]{2,1,0:T(8,128)(2,1)}, u32[]{:S(2)}, u32[]{:S(2)}) collective-permute-start(bf16[48,192,128]{2,1,0:T(8,128)(2,1)} %collective-permute-done.2), channel_id=1, source_target_pairs={{1,2},{2,1},{5,6},{6,5},{9,10},{10,9},{13,14},{14,13},{17,18},{18,... | collective-permute-start | bytes 7077896 | tf_op jit(solution)/shard_map/ppermute | solution.py:162
  295.4 165.2 %collective-permute-start.10 = (bf16[48,192,128]{2,1,0:T(8,128)(2,1)}, bf16[48,192,128]{2,1,0:T(8,128)(2,1)}, u32[]{:S(2)}, u32[]{:S(2)}) collective-permute-start(bf16[48,192,128]{2,1,0:T(8,128)(2,1)} %collective-permute-done.1), channel_id=1, source_target_pairs={{1,2},{2,1},{5,6},{6,5},{9,10},{10,9},{13,14},{14,13},{17,18},{18,... | collective-permute-start | bytes 7077896 | tf_op jit(solution)/shard_map/ppermute | solution.py:162
  307.7 202.7 %collective-permute-start.5 = (bf16[48,192,128]{2,1,0:T(8,128)(2,1)}, bf16[48,192,128]{2,1,0:T(8,128)(2,1)}, u32[]{:S(2)}, u32[]{:S(2)}) collective-permute-start(bf16[48,192,128]{2,1,0:T(8,128)(2,1)} %collective-permute-done), channel_id=1, source_target_pairs={{1,2},{2,1},{5,6},{6,5},{9,10},{10,9},{13,14},{14,13},{17,18},{18,... | collective-permute-start | bytes 7077896 | tf_op jit(solution)/shard_map/ppermute | solution.py:162
  410.0 161.0 %collective-permute-start.21 = (bf16[2,48,192,128]{3,2,1,0:T(8,128)(2,1)}, bf16[2,48,192,128]{3,2,1,0:T(8,128)(2,1)}, u32[]{:S(2)}, u32[]{:S(2)}) collective-permute-start(bf16[2,48,192,128]{3,2,1,0:T(8,128)(2,1)} %copy.107), channel_id=1, source_target_pairs={{0,4},{4,0},{8,12},{12,8},{1,5},{5,1},{9,13},{13,9},{2,6},{6,2},{1... | collective-permute-start | bytes 14155784 | tf_op jit(solution)/shard_map/ppermute | solution.py:117
  460.1 137.3 %collective-permute-start.16 = (bf16[2,48,192,128]{3,2,1,0:T(8,128)(2,1)}, bf16[2,48,192,128]{3,2,1,0:T(8,128)(2,1)}, u32[]{:S(2)}, u32[]{:S(2)}) collective-permute-start(bf16[2,48,192,128]{3,2,1,0:T(8,128)(2,1)} %copy.97), channel_id=1, source_target_pairs={{0,4},{4,0},{8,12},{12,8},{1,5},{5,1},{9,13},{13,9},{2,6},{6,2},{1... | collective-permute-start | bytes 14155784 | tf_op jit(solution)/shard_map/ppermute | solution.py:117
  510.4 115.9 %collective-permute-start.11 = (bf16[2,48,192,128]{3,2,1,0:T(8,128)(2,1)}, bf16[2,48,192,128]{3,2,1,0:T(8,128)(2,1)}, u32[]{:S(2)}, u32[]{:S(2)}) collective-permute-start(bf16[2,48,192,128]{3,2,1,0:T(8,128)(2,1)} %copy.87), channel_id=1, source_target_pairs={{0,4},{4,0},{8,12},{12,8},{1,5},{5,1},{9,13},{13,9},{2,6},{6,2},{1... | collective-permute-start | bytes 14155784 | tf_op jit(solution)/shard_map/ppermute | solution.py:117
  560.5 92.1 %collective-permute-start.6 = (bf16[2,48,192,128]{3,2,1,0:T(8,128)(2,1)}, bf16[2,48,192,128]{3,2,1,0:T(8,128)(2,1)}, u32[]{:S(2)}, u32[]{:S(2)}) collective-permute-start(bf16[2,48,192,128]{3,2,1,0:T(8,128)(2,1)} %copy.77), channel_id=1, source_target_pairs={{0,4},{4,0},{8,12},{12,8},{1,5},{5,1},{9,13},{13,9},{2,6},{6,2},{1... | collective-permute-start | bytes 14155784 | tf_op jit(solution)/shard_map/ppermute | solution.py:117
  595.9 83.2 %collective-permute-start.22 = (bf16[48,192,128]{2,1,0:T(8,128)(2,1)}, bf16[48,192,128]{2,1,0:T(8,128)(2,1)}, u32[]{:S(2)}, u32[]{:S(2)}) collective-permute-start(bf16[48,192,128]{2,1,0:T(8,128)(2,1)} %bitcast.56), channel_id=1, source_target_pairs={{0,8},{8,0},{4,12},{12,4},{1,9},{9,1},{5,13},{13,5},{2,10},{10,2},... | collective-permute-start | bytes 7077896 | tf_op jit(solution)/shard_map/ppermute | solution.py:121
  622.3 129.1 %collective-permute-start.17 = (bf16[48,192,128]{2,1,0:T(8,128)(2,1)}, bf16[48,192,128]{2,1,0:T(8,128)(2,1)}, u32[]{:S(2)}, u32[]{:S(2)}) collective-permute-start(bf16[48,192,128]{2,1,0:T(8,128)(2,1)} %bitcast.191), channel_id=1, source_target_pairs={{0,8},{8,0},{4,12},{12,4},{1,9},{9,1},{5,13},{13,5},{2,10},{10,2},... | collective-permute-start | bytes 7077896 | tf_op jit(solution)/shard_map/ppermute | solution.py:121
  651.1 201.4 %collective-permute-start.12 = (bf16[48,192,128]{2,1,0:T(8,128)(2,1)}, bf16[48,192,128]{2,1,0:T(8,128)(2,1)}, u32[]{:S(2)}, u32[]{:S(2)}) collective-permute-start(bf16[48,192,128]{2,1,0:T(8,128)(2,1)} %bitcast.28), channel_id=1, source_target_pairs={{0,8},{8,0},{4,12},{12,4},{1,9},{9,1},{5,13},{13,5},{2,10},{10,2},... | collective-permute-start | bytes 7077896 | tf_op jit(solution)/shard_map/ppermute | solution.py:121
  678.5 274.2 %collective-permute-start.7 = (bf16[48,192,128]{2,1,0:T(8,128)(2,1)}, bf16[48,192,128]{2,1,0:T(8,128)(2,1)}, u32[]{:S(2)}, u32[]{:S(2)}) collective-permute-start(bf16[48,192,128]{2,1,0:T(8,128)(2,1)} %bitcast.14), channel_id=1, source_target_pairs={{0,8},{8,0},{4,12},{12,4},{1,9},{9,1},{5,13},{13,5},{2,10},{10,2},... | collective-permute-start | bytes 7077896 | tf_op jit(solution)/shard_map/ppermute | solution.py:121
  687.6 68.7 %copy-start.9 = (bf16[48,192,128]{1,0,2:T(8,128)(2,1)}, bf16[48,192,128]{1,0,2:T(8,128)(2,1)S(1)}, u32[]{:S(2)}) copy-start(bf16[48,192,128]{1,0,2:T(8,128)(2,1)S(1)} %fusion.44) | copy-start | bytes 7077892
  691.3 275.6 %collective-permute-start.23 = (bf16[48,192,128]{2,1,0:T(8,128)(2,1)}, bf16[48,192,128]{2,1,0:T(8,128)(2,1)}, u32[]{:S(2)}, u32[]{:S(2)}) collective-permute-start(bf16[48,192,128]{2,1,0:T(8,128)(2,1)} %copy.111), channel_id=1, source_target_pairs={{8,1},{12,5},{1,9},{5,13},{9,8},{13,12},{2,6},{6,2},{10,7},{14,3},... | collective-permute-start | bytes 7077896 | tf_op jit(solution)/shard_map/ppermute | solution.py:188
  766.7 205.4 %collective-permute-start.18 = (bf16[48,192,128]{2,1,0:T(8,128)(2,1)}, bf16[48,192,128]{2,1,0:T(8,128)(2,1)}, u32[]{:S(2)}, u32[]{:S(2)}) collective-permute-start(bf16[48,192,128]{2,1,0:T(8,128)(2,1)} %copy.101), channel_id=1, source_target_pairs={{8,1},{12,5},{1,9},{5,13},{9,8},{13,12},{2,6},{6,2},{10,7},{14,3},... | collective-permute-start | bytes 7077896 | tf_op jit(solution)/shard_map/ppermute | solution.py:188
  861.1 10.8 %copy-start.12 = (bf16[48,192,128]{1,0,2:T(8,128)(2,1)}, bf16[48,192,128]{1,0,2:T(8,128)(2,1)S(1)}, u32[]{:S(2)}) copy-start(bf16[48,192,128]{1,0,2:T(8,128)(2,1)S(1)} %fusion.46) | copy-start | bytes 7077892
  864.8 119.6 %collective-permute-start.13 = (bf16[48,192,128]{2,1,0:T(8,128)(2,1)}, bf16[48,192,128]{2,1,0:T(8,128)(2,1)}, u32[]{:S(2)}, u32[]{:S(2)}) collective-permute-start(bf16[48,192,128]{2,1,0:T(8,128)(2,1)} %copy.91), channel_id=1, source_target_pairs={{8,1},{12,5},{1,9},{5,13},{9,8},{13,12},{2,6},{6,2},{10,7},{14,3},... | collective-permute-start | bytes 7077896 | tf_op jit(solution)/shard_map/ppermute | solution.py:188
  965.0 55.4 %collective-permute-start.8 = (bf16[48,192,128]{2,1,0:T(8,128)(2,1)}, bf16[48,192,128]{2,1,0:T(8,128)(2,1)}, u32[]{:S(2)}, u32[]{:S(2)}) collective-permute-start(bf16[48,192,128]{2,1,0:T(8,128)(2,1)} %copy.81), channel_id=1, source_target_pairs={{8,1},{12,5},{1,9},{5,13},{9,8},{13,12},{2,6},{6,2},{10,7},{14,3},... | collective-permute-start | bytes 7077896 | tf_op jit(solution)/shard_map/ppermute | solution.py:188
  1043.8 10.8 %copy-start.18 = (bf16[192,48,128]{0,1,2:T(8,128)(2,1)S(1)}, bf16[192,48,128]{0,1,2:T(8,128)(2,1)}, u32[]{:S(2)}) copy-start(bf16[192,48,128]{0,1,2:T(8,128)(2,1)} %get-tuple-element.48) | copy-start | bytes 7077892
  (36 other events, 160.6 us)
